TPU v7x, 32 devices: a whole 2x2x4 slice. The times are simulated.
32 devices in a mesh: contact: 8 (over y, x, core), body: 4 (over z).
Axes of the slice: x: 2, y: 2, z: 4, core: 2. Of those that a mesh axis runs over, the one named last changes fastest.
Arguments:
- jacobian: bfloat16 [512, 2, 384, 384], P(('contact', 'body')), may hold values from -0.21875 to 0.21875
- tile_block: int32 [512, 2], P(('contact', 'body')), may hold values from 0 to 31
- tile_count: int32 [32], P(('contact', 'body')), may hold values from 8 to 16, as said below
- vel_free: float32 [128, 384], P('body'), may hold values from -6 to 6
- inv_mass: float32 [128, 384], P('body'), may hold values from 0.25 to 2
- bias: float32 [512, 384], P(('contact', 'body')), may hold values from -6 to 6
- step_scale: float32 [512, 384], P(('contact', 'body')), may hold values from 0.05 to 0.5
- friction: float32 [512, 128], P(('contact', 'body')), may hold values from 0.2 to 1
- impulse_start: float32 [512, 384], P(('contact', 'body')), may hold values from -6 to 6
Outputs:
- impulse: float32 [512, 384], P(('contact', 'body'))
- velocity: float32 [128, 384], P('body')
Inputs may be any that keep to these rules, and one draw needn't show every extreme that they name: `tile_count`: some device has all 16 tile slots live in every draw.
All inputs are finite; a program needn't handle non-finite values.
Results may differ from a plain program's by a relative error of at most 0.0062.
Values may be sent and summed in bfloat16 or wider, within the bound.
No kernel may reach another device: no remote copies, remote signals or barrier semaphores. Data moves between devices by JAX's collectives and lax.ppermute only.
A program may use at most 64 MiB of HBM per device.

v0:
```python
import jax
import jax.numpy as jnp
from jax import lax
from jax.sharding import PartitionSpec as P

ITERS = 2


def shifted(value, axis, steps):
    count = lax.axis_size(axis)
    pairs = [(source, (source + steps) % count) for source in range(count)]
    return lax.ppermute(value, axis, pairs)


def project(trial, friction, contacts):
    normal = trial[:, :contacts]
    first = trial[:, contacts : 2 * contacts]
    second = trial[:, 2 * contacts :]
    tangent = jnp.sqrt(first * first + second * second)
    inside = tangent <= friction * normal
    below = friction * tangent <= -normal
    moved = (normal + friction * tangent) / (1.0 + friction * friction)
    safe = jnp.where(inside | below, 1.0, tangent)
    factor = jnp.where(inside, 1.0, jnp.where(below, 0.0, friction * moved / safe))
    new_normal = jnp.where(inside, normal, jnp.where(below, 0.0, moved))
    return jnp.concatenate([new_normal, first * factor, second * factor], axis=1)


def per_device(
    jacobian, tile_block, tile_count, vel_free, inv_mass, bias, step_scale, friction, impulse_start
):
    tiles_here = jacobian.shape[0]
    slab_blocks = vel_free.shape[0]
    contacts = friction.shape[1]
    order = jnp.arange(tiles_here, dtype=jnp.int32)
    mask = (order < tile_count[0]).astype(jnp.float32)[:, None]
    span = jnp.arange(slab_blocks, dtype=jnp.int32)
    pick_own = (tile_block[:, 0:1] == span[None, :]).astype(jnp.float32)
    pick_next = (tile_block[:, 1:2] == span[None, :]).astype(jnp.float32)
    pick_own_b = pick_own.astype(jnp.bfloat16)
    pick_next_b = pick_next.astype(jnp.bfloat16)

    def merged_partials(lam):
        lamb = lam.astype(jnp.bfloat16)
        push = jnp.einsum("tkbc,tc->tkb", jacobian, lamb, preferred_element_type=jnp.float32)
        own = jnp.einsum("ts,tb->sb", pick_own, push[:, 0], precision=lax.Precision.HIGHEST)
        later = jnp.einsum("ts,tb->sb", pick_next, push[:, 1], precision=lax.Precision.HIGHEST)
        return own + shifted(later, "body", 1)

    def slab_total(lam):
        return lax.psum(merged_partials(lam), "contact")

    lam = impulse_start * mask
    for sweep in range(ITERS):
        total = slab_total(lam)
        velb = (vel_free + inv_mass * total).astype(jnp.bfloat16)
        velb_next = shifted(velb, "body", -1)
        rows_own = jnp.dot(pick_own_b, velb, preferred_element_type=jnp.float32).astype(
            jnp.bfloat16
        )
        rows_next = jnp.dot(pick_next_b, velb_next, preferred_element_type=jnp.float32).astype(
            jnp.bfloat16
        )
        rows = jnp.stack([rows_own, rows_next], axis=1)
        rel = jnp.einsum("tkbc,tkb->tc", jacobian, rows, preferred_element_type=jnp.float32) + bias
        lam = project(lam - step_scale * rel, friction, contacts) * mask
    total = slab_total(lam)
    velocity = vel_free + inv_mass * total
    return (lam, velocity)


def solution(mesh):
    placed = (
        P(("contact", "body"), None, None, None),
        P(("contact", "body"), None),
        P(("contact", "body")),
        P("body", None),
        P("body", None),
        P(("contact", "body"), None),
        P(("contact", "body"), None),
        P(("contact", "body"), None),
        P(("contact", "body"), None),
    )
    return jax.shard_map(
        per_device,
        mesh=mesh,
        in_specs=placed,
        out_specs=(P(("contact", "body"), None), P("body", None)),
        check_vma=False,
    )
```

profile of v0, /device:TPU:0, one launch (start us, length us, event | category | flops | bytes accessed | tf_op | source)
XLA Modules:
  0.0 131.8 jit_solution(11476229442422645573)
XLA Ops:
  0.6 0.0 copy-start.1
  0.6 0.0 copy-start
  1.3 0.8 slice_bitcast_fusion.1
  2.1 0.8 fusion.35
  2.9 0.0 copy-start.2
  2.9 0.0 copy-start.3
  2.9 0.0 copy-start.4
  2.9 0.0 copy-start.5
  2.9 6.2 %fusion.31 = f32[16,1,2,384]{3,1,2,0:T(1,128)S(1)} fusion(bf16[16,2,384,384]{3,2,1,0:T(8,128)(2,1)} %param.9, bf16[16,384,1,1]{1,0,2,3:T(8,128)(2,1)S(1)} %fusion.35), kind=kOutput, calls=%fused_computation.50 | convolution fusion | flops 9437184 | bytes 9498624 | tf_op jit(solution)/shard_map/tkbc,tc->tkb/dot_general | solution.py:45
  9.3 0.3 fusion.18
  9.6 3.1 %collective-permute-start = (f32[32,384]{1,0:T(8,128)S(1)}, f32[32,384]{1,0:T(8,128)S(1)}, u32[]{:S(2)}, u32[]{:S(2)}) collective-permute-start(f32[32,384]{1,0:T(8,128)S(1)} %fusion.18), channel_id=1, source_target_pairs={{0,1},{1,2},{2,3},{3,0},{4,5},{5,6},{6,7},{7,4},{8,9},{9,10},{10,1... | collective-permute-start | bytes 147464 | tf_op jit(solution)/shard_map/ppermute | solution.py:12
  12.6 4.1 %collective-permute-done = f32[32,384]{1,0:T(8,128)S(1)} collective-permute-done((f32[32,384]{1,0:T(8,128)S(1)}, f32[32,384]{1,0:T(8,128)S(1)}, u32[]{:S(2)}, u32[]{:S(2)}) %collective-permute-start) | collective-permute-done | bytes 49184 | tf_op jit(solution)/shard_map/ppermute | solution.py:12
  16.7 0.3 convolution_add_fusion.2
  17.0 23.7 %psum.21 = f32[32,384]{1,0:T(8,128)S(1)} all-reduce(f32[32,384]{1,0:T(8,128)S(1)} %convolution_add_fusion.2), channel_id=1, replica_groups=mesh['contact'=8,'body'=4] {'contact'}, use_global_device_ids=true, to_apply=%region_0.0 | all-reduce | flops 12288 | bytes 98304 | tf_op jit(solution)/shard_map/psum | solution.py:51
  40.7 0.0 copy-done.1
  40.7 0.0 copy-done
  40.7 1.8 %collective-permute-start.1 = (bf16[32,384]{1,0:T(8,128)(2,1)S(1)}, bf16[32,384]{1,0:T(8,128)(2,1)S(1)}, u32[]{:S(2)}, u32[]{:S(2)}) collective-permute-start(bf16[32,384]{1,0:T(8,128)(2,1)S(1)} %add_convert_fusion.1), channel_id=1, source_target_pairs={{0,3},{1,0},{2,1},{3,2},{4,7},{5,4},{6,5},{7,6},{8,11},{9,8},{10,9... | collective-permute-start | bytes 73736 | tf_op jit(solution)/shard_map/ppermute | solution.py:12
  42.5 0.2 fusion
  42.7 1.9 %collective-permute-done.1 = bf16[32,384]{1,0:T(8,128)(2,1)S(1)} collective-permute-done((bf16[32,384]{1,0:T(8,128)(2,1)S(1)}, bf16[32,384]{1,0:T(8,128)(2,1)S(1)}, u32[]{:S(2)}, u32[]{:S(2)}) %collective-permute-start.1) | collective-permute-done | bytes 24608 | tf_op jit(solution)/shard_map/ppermute | solution.py:12
  44.6 0.2 fusion.1
  44.8 5.0 %fusion.6 = f32[16,1,384,1]{2,1,3,0:T(1,128)S(1)} fusion(bf16[16,2,384,384]{3,2,1,0:T(8,128)(2,1)} %param.9, bf16[16,2,384,1]{2,0,1,3:T(8,128)(2,1)S(1)} %maximum_bitcast_fusion), kind=kOutput, calls=%fused_computation.15 | convolution fusion | flops 9437184 | bytes 9486336 | tf_op jit(solution)/shard_map/tkbc,tkb->tc/dot_general | solution.py:65
  49.8 0.0 copy-done.2
  49.9 0.0 copy-done.3
  49.9 0.0 copy-done.4
  49.9 0.1 fusion.26
  49.9 0.0 copy-done.5
  50.0 0.1 fusion.34
  50.1 6.2 %fusion.29 = f32[16,1,2,384]{3,1,2,0:T(1,128)S(1)} fusion(bf16[16,2,384,384]{3,2,1,0:T(8,128)(2,1)} %param.9, bf16[16,384,1,1]{1,0,2,3:T(8,128)(2,1)S(1)} %fusion.34), kind=kOutput, calls=%fused_computation.48 | convolution fusion | flops 9437184 | bytes 9498624 | tf_op jit(solution)/shard_map/tkbc,tc->tkb/dot_general | solution.py:45
  56.4 0.3 fusion.13
  56.7 0.1 collective-permute-start.2
  56.7 5.9 %collective-permute-done.2 = f32[32,384]{1,0:T(8,128)S(1)} collective-permute-done((f32[32,384]{1,0:T(8,128)S(1)}, f32[32,384]{1,0:T(8,128)S(1)}, u32[]{:S(2)}, u32[]{:S(2)}) %collective-permute-start.2) | collective-permute-done | bytes 49184 | tf_op jit(solution)/shard_map/ppermute | solution.py:12
  62.6 0.3 convolution_add_fusion.1
  62.9 22.8 %psum.22 = f32[32,384]{1,0:T(8,128)S(1)} all-reduce(f32[32,384]{1,0:T(8,128)S(1)} %convolution_add_fusion.1), channel_id=1, replica_groups=mesh['contact'=8,'body'=4] {'contact'}, use_global_device_ids=true, to_apply=%region_1.2 | all-reduce | flops 12288 | bytes 98304 | tf_op jit(solution)/shard_map/psum | solution.py:51
  85.7 1.8 %collective-permute-start.3 = (bf16[32,384]{1,0:T(8,128)(2,1)S(1)}, bf16[32,384]{1,0:T(8,128)(2,1)S(1)}, u32[]{:S(2)}, u32[]{:S(2)}) collective-permute-start(bf16[32,384]{1,0:T(8,128)(2,1)S(1)} %add_convert_fusion), channel_id=1, source_target_pairs={{0,3},{1,0},{2,1},{3,2},{4,7},{5,4},{6,5},{7,6},{8,11},{9,8},{10,9... | collective-permute-start | bytes 73736 | tf_op jit(solution)/shard_map/ppermute | solution.py:12
  87.4 0.2 fusion.2
  87.6 1.9 %collective-permute-done.3 = bf16[32,384]{1,0:T(8,128)(2,1)S(1)} collective-permute-done((bf16[32,384]{1,0:T(8,128)(2,1)S(1)}, bf16[32,384]{1,0:T(8,128)(2,1)S(1)}, u32[]{:S(2)}, u32[]{:S(2)}) %collective-permute-start.3) | collective-permute-done | bytes 24608 | tf_op jit(solution)/shard_map/ppermute | solution.py:12
  89.5 0.2 fusion.3
  89.7 5.0 %fusion.4 = f32[16,1,384,1]{2,1,3,0:T(1,128)S(1)} fusion(bf16[16,2,384,384]{3,2,1,0:T(8,128)(2,1)} %param.9, bf16[16,2,384,1]{2,0,1,3:T(8,128)(2,1)S(1)} %maximum_bitcast_fusion.1), kind=kOutput, calls=%fused_computation.12 | convolution fusion | flops 9437184 | bytes 9486336 | tf_op jit(solution)/shard_map/tkbc,tkb->tc/dot_general | solution.py:65
  94.8 0.1 fusion.24
  94.9 0.7 convert_bitcast_fusion
  95.6 6.2 %fusion.27 = f32[16,1,2,384]{3,1,2,0:T(1,128)S(1)} fusion(bf16[16,2,384,384]{3,2,1,0:T(8,128)(2,1)} %param.9, bf16[16,384,1,1]{1,0,2,3:T(8,128)(2,1)S(1)} %get-tuple-element.2), kind=kOutput, calls=%fused_computation.46 | convolution fusion | flops 9437184 | bytes 9498624 | tf_op jit(solution)/shard_map/tkbc,tc->tkb/dot_general | solution.py:45
  101.9 0.3 fusion.8
  102.2 0.1 collective-permute-start.4
  102.3 5.9 %collective-permute-done.4 = f32[32,384]{1,0:T(8,128)S(1)} collective-permute-done((f32[32,384]{1,0:T(8,128)S(1)}, f32[32,384]{1,0:T(8,128)S(1)}, u32[]{:S(2)}, u32[]{:S(2)}) %collective-permute-start.4) | collective-permute-done | bytes 49184 | tf_op jit(solution)/shard_map/ppermute | solution.py:12
  108.1 0.3 convolution_add_fusion
  108.4 22.8 %psum.23 = f32[32,384]{1,0:T(8,128)S(1)} all-reduce(f32[32,384]{1,0:T(8,128)S(1)} %convolution_add_fusion), channel_id=1, replica_groups=mesh['contact'=8,'body'=4] {'contact'}, use_global_device_ids=true, to_apply=%region_2.3 | all-reduce | flops 12288 | bytes 98304 | tf_op jit(solution)/shard_map/psum | solution.py:51
  131.2 0.6 multiply_add_fusion
  (15 shorter events, 0.3 us)
Async XLA Ops:
  0.6 40.0 %copy-start.1 = (f32[32,384]{1,0:T(8,128)S(1)}, f32[32,384]{1,0:T(8,128)}, u32[]{:S(2)}) copy-start(f32[32,384]{1,0:T(8,128)} %param.13) | copy-start | bytes 147460
  0.6 40.0 %copy-start = (f32[32,384]{1,0:T(8,128)S(1)}, f32[32,384]{1,0:T(8,128)}, u32[]{:S(2)}) copy-start(f32[32,384]{1,0:T(8,128)} %param.12) | copy-start | bytes 147460
  2.9 47.0 %copy-start.2 = (f32[16,384]{1,0:T(8,128)S(1)}, f32[16,384]{1,0:T(8,128)}, u32[]{:S(2)}) copy-start(f32[16,384]{1,0:T(8,128)} %param.17) | copy-start | bytes 73732
  2.9 47.0 %copy-start.3 = (f32[16,384]{1,0:T(8,128)S(1)}, f32[16,384]{1,0:T(8,128)}, u32[]{:S(2)}) copy-start(f32[16,384]{1,0:T(8,128)} %param.15) | copy-start | bytes 73732
  2.9 47.0 %copy-start.4 = (f32[16,384]{1,0:T(8,128)S(1)}, f32[16,384]{1,0:T(8,128)}, u32[]{:S(2)}) copy-start(f32[16,384]{1,0:T(8,128)} %param.14) | copy-start | bytes 73732
  2.9 47.0 %copy-start.5 = (f32[16,128]{1,0:T(8,128)S(1)}, f32[16,128]{1,0:T(8,128)}, u32[]{:S(2)}) copy-start(f32[16,128]{1,0:T(8,128)} %param.16) | copy-start | bytes 24580
  9.6 7.2 %collective-permute-start = (f32[32,384]{1,0:T(8,128)S(1)}, f32[32,384]{1,0:T(8,128)S(1)}, u32[]{:S(2)}, u32[]{:S(2)}) collective-permute-start(f32[32,384]{1,0:T(8,128)S(1)} %fusion.18), channel_id=1, source_target_pairs={{0,1},{1,2},{2,3},{3,0},{4,5},{5,6},{6,7},{7,4},{8,9},{9,10},{10,1... | collective-permute-start | bytes 147464 | tf_op jit(solution)/shard_map/ppermute | solution.py:12
  40.7 3.9 %collective-permute-start.1 = (bf16[32,384]{1,0:T(8,128)(2,1)S(1)}, bf16[32,384]{1,0:T(8,128)(2,1)S(1)}, u32[]{:S(2)}, u32[]{:S(2)}) collective-permute-start(bf16[32,384]{1,0:T(8,128)(2,1)S(1)} %add_convert_fusion.1), channel_id=1, source_target_pairs={{0,3},{1,0},{2,1},{3,2},{4,7},{5,4},{6,5},{7,6},{8,11},{9,8},{10,9... | collective-permute-start | bytes 73736 | tf_op jit(solution)/shard_map/ppermute | solution.py:12
  56.7 5.9 %collective-permute-start.2 = (f32[32,384]{1,0:T(8,128)S(1)}, f32[32,384]{1,0:T(8,128)S(1)}, u32[]{:S(2)}, u32[]{:S(2)}) collective-permute-start(f32[32,384]{1,0:T(8,128)S(1)} %fusion.13), channel_id=1, source_target_pairs={{0,1},{1,2},{2,3},{3,0},{4,5},{5,6},{6,7},{7,4},{8,9},{9,10},{10,1... | collective-permute-start | bytes 147464 | tf_op jit(solution)/shard_map/ppermute | solution.py:12
  85.7 3.9 %collective-permute-start.3 = (bf16[32,384]{1,0:T(8,128)(2,1)S(1)}, bf16[32,384]{1,0:T(8,128)(2,1)S(1)}, u32[]{:S(2)}, u32[]{:S(2)}) collective-permute-start(bf16[32,384]{1,0:T(8,128)(2,1)S(1)} %add_convert_fusion), channel_id=1, source_target_pairs={{0,3},{1,0},{2,1},{3,2},{4,7},{5,4},{6,5},{7,6},{8,11},{9,8},{10,9... | collective-permute-start | bytes 73736 | tf_op jit(solution)/shard_map/ppermute | solution.py:12
  102.2 5.9 %collective-permute-start.4 = (f32[32,384]{1,0:T(8,128)S(1)}, f32[32,384]{1,0:T(8,128)S(1)}, u32[]{:S(2)}, u32[]{:S(2)}) collective-permute-start(f32[32,384]{1,0:T(8,128)S(1)} %fusion.8), channel_id=1, source_target_pairs={{0,1},{1,2},{2,3},{3,0},{4,5},{5,6},{6,7},{7,4},{8,9},{9,10},{10,1... | collective-permute-start | bytes 147464 | tf_op jit(solution)/shard_map/ppermute | solution.py:12
where the time goes:
time: 132 us
  blocking collectives  69.2 us (52%)
  matrix products  31.2 us (24%)
  waiting for transfers between devices  19.7 us (15%)
  starting transfers between devices  6.73 us (5%)
  other arithmetic  2.45 us (2%)
  between operations  1.54 us (1%)
    psum x3, blocking collectives, slab_total(): return lax.psum(merged_partials(lam), 'contact')  69.2 us
    ppermute x5, waiting for transfers between devices, shifted(): return lax.ppermute(value, axis, pairs)  19.7 us
    dot_general x3, matrix products, merged_partials(): jnp.einsum('tkbc,tc->tkb', jacobian, lamb, preferred_element_type=jnp.flo...  18.7 us
    dot_general x2, matrix products, per_device(): jnp.einsum('tkbc,tkb->tc', jacobian, rows, preferred_element_type=jnp.flo...  10.1 us
    ppermute x5, starting transfers between devices, shifted(): return lax.ppermute(value, axis, pairs)  6.73 us
  transfers between devices with their start and end apart: 5, of which 5 were waited for; matrix products, arithmetic and copies ran while one was open for 0% of the time, Pallas kernels for 0%

commit v1 on v0

--- a/solution.py
+++ b/solution.py
@@ -10,6 +10,18 @@
     count = lax.axis_size(axis)
     pairs = [(source, (source + steps) % count) for source in range(count)]
     return lax.ppermute(value, axis, pairs)
+
+
+def summed(value, axis):
+    count = lax.axis_size(axis)
+    if count & (count - 1):
+        return lax.psum(value, axis)
+    bit = 1
+    while bit < count:
+        pairs = [(source, source ^ bit) for source in range(count)]
+        value = value + lax.ppermute(value, axis, pairs)
+        bit *= 2
+    return value
 
 
 def project(trial, friction, contacts):
@@ -39,32 +51,35 @@
     pick_next = (tile_block[:, 1:2] == span[None, :]).astype(jnp.float32)
     pick_own_b = pick_own.astype(jnp.bfloat16)
     pick_next_b = pick_next.astype(jnp.bfloat16)
+    free_pair = jnp.concatenate([vel_free, shifted(vel_free, "body", -1)])
+    mass_pair = jnp.concatenate([inv_mass, shifted(inv_mass, "body", -1)])
 
-    def merged_partials(lam):
+    def partials(lam):
         lamb = lam.astype(jnp.bfloat16)
         push = jnp.einsum("tkbc,tc->tkb", jacobian, lamb, preferred_element_type=jnp.float32)
         own = jnp.einsum("ts,tb->sb", pick_own, push[:, 0], precision=lax.Precision.HIGHEST)
         later = jnp.einsum("ts,tb->sb", pick_next, push[:, 1], precision=lax.Precision.HIGHEST)
-        return own + shifted(later, "body", 1)
-
-    def slab_total(lam):
-        return lax.psum(merged_partials(lam), "contact")
+        return own, later
 
     lam = impulse_start * mask
     for sweep in range(ITERS):
-        total = slab_total(lam)
-        velb = (vel_free + inv_mass * total).astype(jnp.bfloat16)
-        velb_next = shifted(velb, "body", -1)
-        rows_own = jnp.dot(pick_own_b, velb, preferred_element_type=jnp.float32).astype(
-            jnp.bfloat16
+        own, later = partials(lam)
+        both = jnp.concatenate(
+            [own + shifted(later, "body", 1), later + shifted(own, "body", -1)]
         )
-        rows_next = jnp.dot(pick_next_b, velb_next, preferred_element_type=jnp.float32).astype(
-            jnp.bfloat16
-        )
+        total = summed(both, "contact")
+        velb = (free_pair + mass_pair * total).astype(jnp.bfloat16)
+        rows_own = jnp.dot(
+            pick_own_b, velb[:slab_blocks], preferred_element_type=jnp.float32
+        ).astype(jnp.bfloat16)
+        rows_next = jnp.dot(
+            pick_next_b, velb[slab_blocks:], preferred_element_type=jnp.float32
+        ).astype(jnp.bfloat16)
         rows = jnp.stack([rows_own, rows_next], axis=1)
         rel = jnp.einsum("tkbc,tkb->tc", jacobian, rows, preferred_element_type=jnp.float32) + bias
         lam = project(lam - step_scale * rel, friction, contacts) * mask
-    total = slab_total(lam)
+    own, later = partials(lam)
+    total = summed(own + shifted(later, "body", 1), "contact")
     velocity = vel_free + inv_mass * total
     return (lam, velocity)
 

time: 132 us -> 83.4 us (0.63)
  blocking collectives: 69.2 us -> 0 us
  waiting for transfers between devices: 19.7 us -> 43.1 us
  matrix products: 31.2 us -> 17.2 us
  starting transfers between devices: 6.73 us -> 18 us
    psum x3 -> x0, blocking collectives: 69.2 us -> none  [slab_total(): return lax.psum(merged_partials(lam), 'contact')]
    ppermute x0 -> x9, waiting for transfers between devices: none -> 22 us  [summed(): value = value + lax.ppermute(value, axis, pairs)]
    ppermute x0 -> x9, starting transfers between devices: none -> 9.48 us  [summed(): value = value + lax.ppermute(value, axis, pairs)]
    dot_general x2, matrix products: 10.1 us -> 2.74 us  [per_device(): jnp.einsum('tkbc,tkb->tc', jacobian, rows, preferred_element_type=jnp.flo...]
    dot_general x13, matrix products: 21.1 us -> 14.5 us  [the longest x3 12 us: partials(): jnp.einsum('tkbc,tc->tkb', jacobian, lamb, preferred_element_type=jnp.flo...]
    ppermute x5 -> x7, starting transfers between devices: 6.73 us -> 8.56 us  [shifted(): return lax.ppermute(value, axis, pairs)]
    ppermute x5 -> x7, waiting for transfers between devices: 19.7 us -> 21.1 us  [shifted(): return lax.ppermute(value, axis, pairs)]
  transfers between devices with their start and end apart: 5 -> 16, of which waited for: 5 -> 14; matrix products, arithmetic and copies ran while one was open for 0% -> 0% of each run, Pallas kernels for 0% -> 0%
where the time goes in v1:
time: 83.4 us; the launch traced here: 83.2 us
  waiting for transfers between devices  43.1 us (52%)
  starting transfers between devices  18 us (22%)
  matrix products  17.2 us (21%)
  other arithmetic  2.76 us (3%)
  between operations  1.76 us (2%)
    ppermute x9, waiting for transfers between devices, summed(): value = value + lax.ppermute(value, axis, pairs)  22 us
    ppermute x7, waiting for transfers between devices, shifted(): return lax.ppermute(value, axis, pairs)  21.1 us
    dot_general x3, matrix products, partials(): jnp.einsum('tkbc,tc->tkb', jacobian, lamb, preferred_element_type=jnp.flo...  12 us
    ppermute x9, starting transfers between devices, summed(): value = value + lax.ppermute(value, axis, pairs)  9.48 us
    ppermute x7, starting transfers between devices, shifted(): return lax.ppermute(value, axis, pairs)  8.56 us
    dot_general x2, matrix products, per_device(): jnp.einsum('tkbc,tkb->tc', jacobian, rows, preferred_element_type=jnp.flo...  2.74 us
    convert_element_type x3, other arithmetic, partials(): lamb = lam.astype(jnp.bfloat16)  1.72 us
  transfers between devices with their start and end apart: 16, of which 14 were waited for; matrix products, arithmetic and copies ran while one was open for 0% of the time, Pallas kernels for 0%

profile of v1, /device:TPU:0, one launch (start us, length us, event | category | flops | bytes accessed | tf_op | source)
XLA Modules:
  0.0 83.2 jit_solution(14840424220074852158)
XLA Ops:
  0.6 0.0 copy-start
  0.6 0.0 copy-start.7
  0.7 0.0 copy-start.1
  0.7 0.0 copy-start.2
  1.5 1.0 %fusion.41 = bf16[16,384,1,1]{1,0,2,3:T(8,128)(2,1)S(1)} fusion(f32[16,384]{1,0:T(8,128)} %param.17, f32[16]{0:T(128)S(1)} %compare_convert_fusion), kind=kLoop, calls=%fused_computation.61 | loop fusion | flops 12288 | bytes 36928 | tf_op jit(solution)/shard_map/convert_element_type | solution.py:58
  2.5 0.0 copy-start.6
  2.5 7.0 %fusion.37 = f32[16,1,2,384]{3,1,2,0:T(1,128)S(1)} fusion(bf16[16,2,384,384]{3,2,1,0:T(8,128)(2,1)} %param.9, bf16[16,384,1,1]{1,0,2,3:T(8,128)(2,1)S(1)} %fusion.41), kind=kOutput, calls=%fused_computation.56 | convolution fusion | flops 9437184 | bytes 9498624 | tf_op jit(solution)/shard_map/tkbc,tc->tkb/dot_general | solution.py:59
  9.5 0.0 copy-done.7
  9.6 0.3 fusion.26
  9.8 5.1 %collective-permute-start.3 = (f32[32,384]{1,0:T(8,128)S(1)}, f32[32,384]{1,0:T(8,128)S(1)}, u32[]{:S(2)}, u32[]{:S(2)}) collective-permute-start(f32[32,384]{1,0:T(8,128)S(1)} %fusion.26), channel_id=1, source_target_pairs={{0,3},{1,0},{2,1},{3,2},{4,7},{5,4},{6,5},{7,6},{8,11},{9,8},{10,9... | collective-permute-start | bytes 147464 | tf_op jit(solution)/shard_map/ppermute | solution.py:12
  15.0 0.0 copy-done.1
  15.0 0.4 collective-permute-start
  15.4 0.0 copy-done.2
  15.4 0.4 collective-permute-start.1
  15.9 1.3 %collective-permute-done.3 = f32[32,384]{1,0:T(8,128)S(1)} collective-permute-done((f32[32,384]{1,0:T(8,128)S(1)}, f32[32,384]{1,0:T(8,128)S(1)}, u32[]{:S(2)}, u32[]{:S(2)}) %collective-permute-start.3) | collective-permute-done | bytes 49184 | tf_op jit(solution)/shard_map/ppermute | solution.py:12
  17.1 0.3 fusion.58
  17.4 0.4 collective-permute-start.2
  17.8 6.0 %collective-permute-done.2 = f32[32,384]{1,0:T(8,128)S(1)} collective-permute-done((f32[32,384]{1,0:T(8,128)S(1)}, f32[32,384]{1,0:T(8,128)S(1)}, u32[]{:S(2)}, u32[]{:S(2)}) %collective-permute-start.2) | collective-permute-done | bytes 49184 | tf_op jit(solution)/shard_map/ppermute | solution.py:12
  23.9 0.1 collective-permute-start.4
  23.9 1.3 %collective-permute-done.4 = f32[64,384]{1,0:T(8,128)S(1)} collective-permute-done((f32[64,384]{1,0:T(8,128)S(1)}, f32[64,384]{1,0:T(8,128)S(1)}, u32[]{:S(2)}, u32[]{:S(2)}) %collective-permute-start.4) | collective-permute-done | bytes 98336 | tf_op jit(solution)/shard_map/ppermute | solution.py:22
  25.2 1.5 %collective-permute-start.5 = (f32[64,384]{1,0:T(8,128)S(1)}, f32[64,384]{1,0:T(8,128)S(1)}, u32[]{:S(2)}, u32[]{:S(2)}) collective-permute-start(f32[64,384]{1,0:T(8,128)S(1)} %fusion.54), channel_id=1, source_target_pairs={{0,8},{4,12},{8,0},{12,4},{16,24},{20,28},{24,16},{28,20},{1,9},{5... | collective-permute-start | bytes 294920 | tf_op jit(solution)/shard_map/ppermute | solution.py:22
  26.8 0.0 collective-permute-done
  26.8 3.4 %collective-permute-done.5 = f32[64,384]{1,0:T(8,128)S(1)} collective-permute-done((f32[64,384]{1,0:T(8,128)S(1)}, f32[64,384]{1,0:T(8,128)S(1)}, u32[]{:S(2)}, u32[]{:S(2)}) %collective-permute-start.5) | collective-permute-done | bytes 98336 | tf_op jit(solution)/shard_map/ppermute | solution.py:22
  30.2 1.6 %collective-permute-start.6 = (f32[64,384]{1,0:T(8,128)S(1)}, f32[64,384]{1,0:T(8,128)S(1)}, u32[]{:S(2)}, u32[]{:S(2)}) collective-permute-start(f32[64,384]{1,0:T(8,128)S(1)} %add.76), channel_id=1, source_target_pairs={{0,16},{4,20},{8,24},{12,28},{16,0},{20,4},{24,8},{28,12},{1,17},{... | collective-permute-start | bytes 294920 | tf_op jit(solution)/shard_map/ppermute | solution.py:22
  31.7 0.0 collective-permute-done.1
  31.7 3.1 %collective-permute-done.6 = f32[64,384]{1,0:T(8,128)S(1)} collective-permute-done((f32[64,384]{1,0:T(8,128)S(1)}, f32[64,384]{1,0:T(8,128)S(1)}, u32[]{:S(2)}, u32[]{:S(2)}) %collective-permute-start.6) | collective-permute-done | bytes 98336 | tf_op jit(solution)/shard_map/ppermute | solution.py:22
  34.9 0.2 fusion.1
  35.1 0.2 fusion
  35.3 0.0 copy-done
  35.3 1.4 %fusion.6 = f32[16,1,384,1]{2,1,3,0:T(1,128)S(1)} fusion(bf16[16,2,384,384]{3,2,1,0:T(8,128)(2,1)S(1)} %copy-done, bf16[16,2,384,1]{2,0,1,3:T(8,128)(2,1)S(1)} %maximum_bitcast_fusion), kind=kOutput, calls=%fused_computation.17 | convolution fusion | flops 9437184 | bytes 9486336 | tf_op jit(solution)/shard_map/tkbc,tkb->tc/dot_general | solution.py:79
  36.7 0.0 copy-done.3
  36.7 0.0 copy-done.5
  36.7 0.1 fusion.32
  36.8 0.1 fusion.40
  36.9 2.5 %fusion.35 = f32[16,1,2,384]{3,1,2,0:T(1,128)S(1)} fusion(bf16[16,2,384,384]{3,2,1,0:T(8,128)(2,1)S(1)} %copy-done, bf16[16,384,1,1]{1,0,2,3:T(8,128)(2,1)S(1)} %fusion.40), kind=kOutput, calls=%fused_computation.54 | convolution fusion | flops 9437184 | bytes 9498624 | tf_op jit(solution)/shard_map/tkbc,tc->tkb/dot_general | solution.py:59
  39.5 0.3 fusion.20
  39.8 2.1 %collective-permute-start.8 = (f32[32,384]{1,0:T(8,128)S(1)}, f32[32,384]{1,0:T(8,128)S(1)}, u32[]{:S(2)}, u32[]{:S(2)}) collective-permute-start(f32[32,384]{1,0:T(8,128)S(1)} %fusion.20), channel_id=1, source_target_pairs={{0,3},{1,0},{2,1},{3,2},{4,7},{5,4},{6,5},{7,6},{8,11},{9,8},{10,9... | collective-permute-start | bytes 147464 | tf_op jit(solution)/shard_map/ppermute | solution.py:12
  41.9 2.1 %collective-permute-done.8 = f32[32,384]{1,0:T(8,128)S(1)} collective-permute-done((f32[32,384]{1,0:T(8,128)S(1)}, f32[32,384]{1,0:T(8,128)S(1)}, u32[]{:S(2)}, u32[]{:S(2)}) %collective-permute-start.8) | collective-permute-done | bytes 49184 | tf_op jit(solution)/shard_map/ppermute | solution.py:12
  43.9 0.3 fusion.59
  44.2 0.1 collective-permute-start.7
  44.3 5.9 %collective-permute-done.7 = f32[32,384]{1,0:T(8,128)S(1)} collective-permute-done((f32[32,384]{1,0:T(8,128)S(1)}, f32[32,384]{1,0:T(8,128)S(1)}, u32[]{:S(2)}, u32[]{:S(2)}) %collective-permute-start.7) | collective-permute-done | bytes 49184 | tf_op jit(solution)/shard_map/ppermute | solution.py:12
  50.2 0.1 collective-permute-start.9
  50.3 1.3 %collective-permute-done.9 = f32[64,384]{1,0:T(8,128)S(1)} collective-permute-done((f32[64,384]{1,0:T(8,128)S(1)}, f32[64,384]{1,0:T(8,128)S(1)}, u32[]{:S(2)}, u32[]{:S(2)}) %collective-permute-start.9) | collective-permute-done | bytes 98336 | tf_op jit(solution)/shard_map/ppermute | solution.py:22
  51.6 1.5 %collective-permute-start.10 = (f32[64,384]{1,0:T(8,128)S(1)}, f32[64,384]{1,0:T(8,128)S(1)}, u32[]{:S(2)}, u32[]{:S(2)}) collective-permute-start(f32[64,384]{1,0:T(8,128)S(1)} %fusion.53), channel_id=1, source_target_pairs={{0,8},{4,12},{8,0},{12,4},{16,24},{20,28},{24,16},{28,20},{1,9},{5... | collective-permute-start | bytes 294920 | tf_op jit(solution)/shard_map/ppermute | solution.py:22
  53.1 3.4 %collective-permute-done.10 = f32[64,384]{1,0:T(8,128)S(1)} collective-permute-done((f32[64,384]{1,0:T(8,128)S(1)}, f32[64,384]{1,0:T(8,128)S(1)}, u32[]{:S(2)}, u32[]{:S(2)}) %collective-permute-start.10) | collective-permute-done | bytes 98336 | tf_op jit(solution)/shard_map/ppermute | solution.py:22
  56.5 1.6 %collective-permute-start.11 = (f32[64,384]{1,0:T(8,128)S(1)}, f32[64,384]{1,0:T(8,128)S(1)}, u32[]{:S(2)}, u32[]{:S(2)}) collective-permute-start(f32[64,384]{1,0:T(8,128)S(1)} %add.86), channel_id=1, source_target_pairs={{0,16},{4,20},{8,24},{12,28},{16,0},{20,4},{24,8},{28,12},{1,17},{... | collective-permute-start | bytes 294920 | tf_op jit(solution)/shard_map/ppermute | solution.py:22
  58.1 3.1 %collective-permute-done.11 = f32[64,384]{1,0:T(8,128)S(1)} collective-permute-done((f32[64,384]{1,0:T(8,128)S(1)}, f32[64,384]{1,0:T(8,128)S(1)}, u32[]{:S(2)}, u32[]{:S(2)}) %collective-permute-start.11) | collective-permute-done | bytes 98336 | tf_op jit(solution)/shard_map/ppermute | solution.py:22
  61.2 0.2 fusion.3
  61.4 0.2 fusion.2
  61.6 1.4 %fusion.4 = f32[16,1,384,1]{2,1,3,0:T(1,128)S(1)} fusion(bf16[16,2,384,384]{3,2,1,0:T(8,128)(2,1)S(1)} %copy-done, bf16[16,2,384,1]{2,0,1,3:T(8,128)(2,1)S(1)} %maximum_bitcast_fusion.1), kind=kOutput, calls=%fused_computation.14 | convolution fusion | flops 9437184 | bytes 9486336 | tf_op jit(solution)/shard_map/tkbc,tkb->tc/dot_general | solution.py:79
  63.0 0.1 fusion.30
  63.1 0.7 convert_bitcast_fusion
  63.8 2.5 %fusion.33 = f32[16,1,2,384]{3,1,2,0:T(1,128)S(1)} fusion(bf16[16,2,384,384]{3,2,1,0:T(8,128)(2,1)S(1)} %copy-done, bf16[16,384,1,1]{1,0,2,3:T(8,128)(2,1)S(1)} %get-tuple-element.2), kind=kOutput, calls=%fused_computation.52 | convolution fusion | flops 9437184 | bytes 9498624 | tf_op jit(solution)/shard_map/tkbc,tc->tkb/dot_general | solution.py:59
  66.4 0.3 fusion.12
  66.7 0.1 collective-permute-start.12
  66.8 5.9 %collective-permute-done.12 = f32[32,384]{1,0:T(8,128)S(1)} collective-permute-done((f32[32,384]{1,0:T(8,128)S(1)}, f32[32,384]{1,0:T(8,128)S(1)}, u32[]{:S(2)}, u32[]{:S(2)}) %collective-permute-start.12) | collective-permute-done | bytes 49184 | tf_op jit(solution)/shard_map/ppermute | solution.py:12
  72.7 0.3 convolution_add_fusion
  73.0 0.1 collective-permute-start.13
  73.0 1.2 %collective-permute-done.13 = f32[32,384]{1,0:T(8,128)S(1)} collective-permute-done((f32[32,384]{1,0:T(8,128)S(1)}, f32[32,384]{1,0:T(8,128)S(1)}, u32[]{:S(2)}, u32[]{:S(2)}) %collective-permute-start.13) | collective-permute-done | bytes 49184 | tf_op jit(solution)/shard_map/ppermute | solution.py:22
  74.3 1.5 %collective-permute-start.14 = (f32[32,384]{1,0:T(8,128)S(1)}, f32[32,384]{1,0:T(8,128)S(1)}, u32[]{:S(2)}, u32[]{:S(2)}) collective-permute-start(f32[32,384]{1,0:T(8,128)S(1)} %add.93), channel_id=1, source_target_pairs={{0,8},{4,12},{8,0},{12,4},{16,24},{20,28},{24,16},{28,20},{1,9},{5... | collective-permute-start | bytes 147464 | tf_op jit(solution)/shard_map/ppermute | solution.py:22
  75.8 2.6 %collective-permute-done.14 = f32[32,384]{1,0:T(8,128)S(1)} collective-permute-done((f32[32,384]{1,0:T(8,128)S(1)}, f32[32,384]{1,0:T(8,128)S(1)}, u32[]{:S(2)}, u32[]{:S(2)}) %collective-permute-start.14) | collective-permute-done | bytes 49184 | tf_op jit(solution)/shard_map/ppermute | solution.py:22
  78.4 1.6 %collective-permute-start.15 = (f32[32,384]{1,0:T(8,128)S(1)}, f32[32,384]{1,0:T(8,128)S(1)}, u32[]{:S(2)}, u32[]{:S(2)}) collective-permute-start(f32[32,384]{1,0:T(8,128)S(1)} %add.94), channel_id=1, source_target_pairs={{0,16},{4,20},{8,24},{12,28},{16,0},{20,4},{24,8},{28,12},{1,17},{... | collective-permute-start | bytes 147464 | tf_op jit(solution)/shard_map/ppermute | solution.py:22
  80.0 2.6 %collective-permute-done.15 = f32[32,384]{1,0:T(8,128)S(1)} collective-permute-done((f32[32,384]{1,0:T(8,128)S(1)}, f32[32,384]{1,0:T(8,128)S(1)}, u32[]{:S(2)}, u32[]{:S(2)}) %collective-permute-start.15) | collective-permute-done | bytes 49184 | tf_op jit(solution)/shard_map/ppermute | solution.py:22
  82.6 0.6 multiply_add_fusion
  (35 shorter events, 0.5 us)
Async XLA Ops:
  0.6 34.7 %copy-start = (bf16[16,2,384,384]{3,2,1,0:T(8,128)(2,1)S(1)}, bf16[16,2,384,384]{3,2,1,0:T(8,128)(2,1)}, u32[]{:S(2)}) copy-start(bf16[16,2,384,384]{3,2,1,0:T(8,128)(2,1)} %param.9) | copy-start | bytes 28311556
  0.6 8.9 %copy-start.7 = (s32[16,2]{0,1:T(2,128)S(1)}, s32[16,2]{0,1:T(2,128)}, u32[]{:S(2)}) copy-start(s32[16,2]{0,1:T(2,128)} %param.10) | copy-start | bytes 388
  0.7 14.3 %copy-start.1 = (f32[32,384]{1,0:T(8,128)S(1)}, f32[32,384]{1,0:T(8,128)}, u32[]{:S(2)}) copy-start(f32[32,384]{1,0:T(8,128)} %param.12) | copy-start | bytes 147460
  0.7 14.7 %copy-start.2 = (f32[32,384]{1,0:T(8,128)S(1)}, f32[32,384]{1,0:T(8,128)}, u32[]{:S(2)}) copy-start(f32[32,384]{1,0:T(8,128)} %param.13) | copy-start | bytes 147460
  2.4 34.2 %copy-start.3 = (f32[16,384]{1,0:T(8,128)S(1)}, f32[16,384]{1,0:T(8,128)}, u32[]{:S(2)}) copy-start(f32[16,384]{1,0:T(8,128)} %param.17) | copy-start | bytes 73732
  2.4 34.2 %copy-start.4 = (f32[16,384]{1,0:T(8,128)S(1)}, f32[16,384]{1,0:T(8,128)}, u32[]{:S(2)}) copy-start(f32[16,384]{1,0:T(8,128)} %param.15) | copy-start | bytes 73732
  2.4 34.2 %copy-start.5 = (f32[16,384]{1,0:T(8,128)S(1)}, f32[16,384]{1,0:T(8,128)}, u32[]{:S(2)}) copy-start(f32[16,384]{1,0:T(8,128)} %param.14) | copy-start | bytes 73732
  2.5 34.3 %copy-start.6 = (f32[16,128]{1,0:T(8,128)S(1)}, f32[16,128]{1,0:T(8,128)}, u32[]{:S(2)}) copy-start(f32[16,128]{1,0:T(8,128)} %param.16) | copy-start | bytes 24580
  9.8 7.3 %collective-permute-start.3 = (f32[32,384]{1,0:T(8,128)S(1)}, f32[32,384]{1,0:T(8,128)S(1)}, u32[]{:S(2)}, u32[]{:S(2)}) collective-permute-start(f32[32,384]{1,0:T(8,128)S(1)} %fusion.26), channel_id=1, source_target_pairs={{0,3},{1,0},{2,1},{3,2},{4,7},{5,4},{6,5},{7,6},{8,11},{9,8},{10,9... | collective-permute-start | bytes 147464 | tf_op jit(solution)/shard_map/ppermute | solution.py:12
  15.0 11.8 %collective-permute-start = (f32[32,384]{1,0:T(8,128)S(1)}, f32[32,384]{1,0:T(8,128)S(1)}, u32[]{:S(2)}, u32[]{:S(2)}) collective-permute-start(f32[32,384]{1,0:T(8,128)S(1)} %copy-done.1), channel_id=1, source_target_pairs={{0,3},{1,0},{2,1},{3,2},{4,7},{5,4},{6,5},{7,6},{8,11},{9,8},{10,9... | collective-permute-start | bytes 147464 | tf_op jit(solution)/shard_map/ppermute | solution.py:12
  15.4 16.3 %collective-permute-start.1 = (f32[32,384]{1,0:T(8,128)S(1)}, f32[32,384]{1,0:T(8,128)S(1)}, u32[]{:S(2)}, u32[]{:S(2)}) collective-permute-start(f32[32,384]{1,0:T(8,128)S(1)} %copy-done.2), channel_id=1, source_target_pairs={{0,3},{1,0},{2,1},{3,2},{4,7},{5,4},{6,5},{7,6},{8,11},{9,8},{10,9... | collective-permute-start | bytes 147464 | tf_op jit(solution)/shard_map/ppermute | solution.py:12
  17.4 6.4 %collective-permute-start.2 = (f32[32,384]{1,0:T(8,128)S(1)}, f32[32,384]{1,0:T(8,128)S(1)}, u32[]{:S(2)}, u32[]{:S(2)}) collective-permute-start(f32[32,384]{1,0:T(8,128)S(1)} %get-tuple-element.19), channel_id=1, source_target_pairs={{0,1},{1,2},{2,3},{3,0},{4,5},{5,6},{6,7},{7,4},{8,9},{9,10},{10,1... | collective-permute-start | bytes 147464 | tf_op jit(solution)/shard_map/ppermute | solution.py:12
  23.9 1.4 %collective-permute-start.4 = (f32[64,384]{1,0:T(8,128)S(1)}, f32[64,384]{1,0:T(8,128)S(1)}, u32[]{:S(2)}, u32[]{:S(2)}) collective-permute-start(f32[64,384]{1,0:T(8,128)S(1)} %pad_maximum_fusion), channel_id=1, source_target_pairs={{0,4},{4,0},{8,12},{12,8},{16,20},{20,16},{24,28},{28,24},{1,5},{5... | collective-permute-start | bytes 294920 | tf_op jit(solution)/shard_map/ppermute | solution.py:22
  25.2 4.9 %collective-permute-start.5 = (f32[64,384]{1,0:T(8,128)S(1)}, f32[64,384]{1,0:T(8,128)S(1)}, u32[]{:S(2)}, u32[]{:S(2)}) collective-permute-start(f32[64,384]{1,0:T(8,128)S(1)} %fusion.54), channel_id=1, source_target_pairs={{0,8},{4,12},{8,0},{12,4},{16,24},{20,28},{24,16},{28,20},{1,9},{5... | collective-permute-start | bytes 294920 | tf_op jit(solution)/shard_map/ppermute | solution.py:22
  30.2 4.7 %collective-permute-start.6 = (f32[64,384]{1,0:T(8,128)S(1)}, f32[64,384]{1,0:T(8,128)S(1)}, u32[]{:S(2)}, u32[]{:S(2)}) collective-permute-start(f32[64,384]{1,0:T(8,128)S(1)} %add.76), channel_id=1, source_target_pairs={{0,16},{4,20},{8,24},{12,28},{16,0},{20,4},{24,8},{28,12},{1,17},{... | collective-permute-start | bytes 294920 | tf_op jit(solution)/shard_map/ppermute | solution.py:22
  39.8 4.1 %collective-permute-start.8 = (f32[32,384]{1,0:T(8,128)S(1)}, f32[32,384]{1,0:T(8,128)S(1)}, u32[]{:S(2)}, u32[]{:S(2)}) collective-permute-start(f32[32,384]{1,0:T(8,128)S(1)} %fusion.20), channel_id=1, source_target_pairs={{0,3},{1,0},{2,1},{3,2},{4,7},{5,4},{6,5},{7,6},{8,11},{9,8},{10,9... | collective-permute-start | bytes 147464 | tf_op jit(solution)/shard_map/ppermute | solution.py:12
  44.2 5.9 %collective-permute-start.7 = (f32[32,384]{1,0:T(8,128)S(1)}, f32[32,384]{1,0:T(8,128)S(1)}, u32[]{:S(2)}, u32[]{:S(2)}) collective-permute-start(f32[32,384]{1,0:T(8,128)S(1)} %get-tuple-element.21), channel_id=1, source_target_pairs={{0,1},{1,2},{2,3},{3,0},{4,5},{5,6},{6,7},{7,4},{8,9},{9,10},{10,1... | collective-permute-start | bytes 147464 | tf_op jit(solution)/shard_map/ppermute | solution.py:12
  50.2 1.4 %collective-permute-start.9 = (f32[64,384]{1,0:T(8,128)S(1)}, f32[64,384]{1,0:T(8,128)S(1)}, u32[]{:S(2)}, u32[]{:S(2)}) collective-permute-start(f32[64,384]{1,0:T(8,128)S(1)} %pad_maximum_fusion.1), channel_id=1, source_target_pairs={{0,4},{4,0},{8,12},{12,8},{16,20},{20,16},{24,28},{28,24},{1,5},{5... | collective-permute-start | bytes 294920 | tf_op jit(solution)/shard_map/ppermute | solution.py:22
  51.6 4.9 %collective-permute-start.10 = (f32[64,384]{1,0:T(8,128)S(1)}, f32[64,384]{1,0:T(8,128)S(1)}, u32[]{:S(2)}, u32[]{:S(2)}) collective-permute-start(f32[64,384]{1,0:T(8,128)S(1)} %fusion.53), channel_id=1, source_target_pairs={{0,8},{4,12},{8,0},{12,4},{16,24},{20,28},{24,16},{28,20},{1,9},{5... | collective-permute-start | bytes 294920 | tf_op jit(solution)/shard_map/ppermute | solution.py:22
  56.5 4.7 %collective-permute-start.11 = (f32[64,384]{1,0:T(8,128)S(1)}, f32[64,384]{1,0:T(8,128)S(1)}, u32[]{:S(2)}, u32[]{:S(2)}) collective-permute-start(f32[64,384]{1,0:T(8,128)S(1)} %add.86), channel_id=1, source_target_pairs={{0,16},{4,20},{8,24},{12,28},{16,0},{20,4},{24,8},{28,12},{1,17},{... | collective-permute-start | bytes 294920 | tf_op jit(solution)/shard_map/ppermute | solution.py:22
  66.7 5.9 %collective-permute-start.12 = (f32[32,384]{1,0:T(8,128)S(1)}, f32[32,384]{1,0:T(8,128)S(1)}, u32[]{:S(2)}, u32[]{:S(2)}) collective-permute-start(f32[32,384]{1,0:T(8,128)S(1)} %fusion.12), channel_id=1, source_target_pairs={{0,1},{1,2},{2,3},{3,0},{4,5},{5,6},{6,7},{7,4},{8,9},{9,10},{10,1... | collective-permute-start | bytes 147464 | tf_op jit(solution)/shard_map/ppermute | solution.py:12
  73.0 1.3 %collective-permute-start.13 = (f32[32,384]{1,0:T(8,128)S(1)}, f32[32,384]{1,0:T(8,128)S(1)}, u32[]{:S(2)}, u32[]{:S(2)}) collective-permute-start(f32[32,384]{1,0:T(8,128)S(1)} %convolution_add_fusion), channel_id=1, source_target_pairs={{0,4},{4,0},{8,12},{12,8},{16,20},{20,16},{24,28},{28,24},{1,5},{5... | collective-permute-start | bytes 147464 | tf_op jit(solution)/shard_map/ppermute | solution.py:22
  74.3 4.2 %collective-permute-start.14 = (f32[32,384]{1,0:T(8,128)S(1)}, f32[32,384]{1,0:T(8,128)S(1)}, u32[]{:S(2)}, u32[]{:S(2)}) collective-permute-start(f32[32,384]{1,0:T(8,128)S(1)} %add.93), channel_id=1, source_target_pairs={{0,8},{4,12},{8,0},{12,4},{16,24},{20,28},{24,16},{28,20},{1,9},{5... | collective-permute-start | bytes 147464 | tf_op jit(solution)/shard_map/ppermute | solution.py:22
  78.4 4.2 %collective-permute-start.15 = (f32[32,384]{1,0:T(8,128)S(1)}, f32[32,384]{1,0:T(8,128)S(1)}, u32[]{:S(2)}, u32[]{:S(2)}) collective-permute-start(f32[32,384]{1,0:T(8,128)S(1)} %add.94), channel_id=1, source_target_pairs={{0,16},{4,20},{8,24},{12,28},{16,0},{20,4},{24,8},{28,12},{1,17},{... | collective-permute-start | bytes 147464 | tf_op jit(solution)/shard_map/ppermute | solution.py:22
